TPU v7x, 32 devices: a whole 2x2x4 slice. The times are simulated.
32 devices in a mesh: dp: 8 (over z, x), group: 4 (over y, core).
Axes of the slice: x: 2, y: 2, z: 4, core: 2. Of those that a mesh axis runs over, the one named last changes fastest.
Arguments:
- train_grads: float32 [32768, 1024], P(('dp', 'group')), may hold values from -50 to 50
- val_grads: float32 [16, 32, 1024], P('dp', 'group'), may hold values from -6 to 6
- wanted: int32 [8, 8], replicated, may hold values from -1 to 15, as said below
- owner: int32 [8], replicated, may hold values from 0 to 7, each once
Outputs:
- scores: float32 [32768, 256], P(('dp', 'group'))
Inputs may be any that keep to these rules, and one draw needn't show every extreme that they name: wanted[b, j] is -1 or the id of a validation block stored on index j of dp, one of j * 2 to j * 2 + 1; training blocks differ in how many slots are used.
All inputs are finite; a program needn't handle non-finite values.
Results may differ from a plain program's by a relative error of at most 0.0003.
Values sent between devices are 32-bit elements; how exact they have to be, the bound alone decides.
A program may use at most 128 MiB of HBM per device.

v0:
```python
import jax
import jax.numpy as jnp
from jax import lax
from jax.sharding import PartitionSpec as P

damping = 0.1


def cholesky_apply(factor, right_side):
    middle = lax.linalg.triangular_solve(factor, right_side, left_side=True, lower=True)
    return lax.linalg.triangular_solve(factor, middle, left_side=True, lower=True, transpose_a=True)


def solve_blocks(factor, blocks_in):
    features = blocks_in.shape[-1]
    flat_rows = blocks_in.reshape(-1, features)
    return cholesky_apply(factor, flat_rows.T).T.reshape(blocks_in.shape)


def local(train_grads, val_grads, wanted, owner):
    highest = lax.Precision.HIGHEST
    partial_gram = lax.dot_general(
        train_grads, train_grads, (((0,), (0,)), ((), ())), precision=highest
    )
    summed = lax.psum(partial_gram, ("dp", "group"))
    features = summed.shape[0]
    rows_total = train_grads.shape[0] * lax.axis_size("dp") * lax.axis_size("group")
    gram_matrix = summed / rows_total + damping * jnp.eye(features, dtype=jnp.float32)
    factor = jnp.linalg.cholesky(gram_matrix)
    blocks = val_grads.shape[0]
    devices = lax.axis_size("dp")
    own_index = lax.axis_index("dp")
    positions = jnp.arange(devices, dtype=jnp.int32)
    holder = jnp.sum(jnp.where(owner[None, :] == positions[:, None], positions[None, :], 0), axis=1)
    requests = wanted[holder]
    column = lax.dynamic_slice_in_dim(requests, own_index, 1, 1)[:, 0]
    local_id = column - own_index * blocks
    chooser = (
        (local_id[:, None] == jnp.arange(blocks, dtype=jnp.int32)[None, :]) & (column[:, None] >= 0)
    ).astype(jnp.float32)
    score_scale = features ** (-0.5)
    source = solve_blocks(factor, val_grads)
    outgoing = jnp.einsum("iv,vqk->iqk", chooser, source, precision=highest)
    arrived = lax.all_to_all(outgoing, "dp", split_axis=0, concat_axis=0, tiled=True)
    tiled = (
        lax.dot_general(
            train_grads,
            lax.all_gather(arrived, "group", axis=1, tiled=True),
            (((1,), (2,)), ((), ())),
            precision=highest,
        )
        * score_scale
    )
    scores = tiled.reshape(train_grads.shape[0], -1)
    return scores


def solution(mesh):
    in_specs = (P(("dp", "group"), None), P("dp", "group", None), P(), P())
    out_specs = P(("dp", "group"), None)
    return jax.shard_map(local, mesh=mesh, in_specs=in_specs, out_specs=out_specs, check_vma=False)
```

profile of v0, /device:TPU:0, one launch (start us, length us, event | category | flops | bytes accessed | tf_op | source)
XLA Modules:
  0.0 564.6 jit_solution(10434394786864650119)
XLA Ops:
  6.5 17.8 %fusion.110 = f32[1024,1024]{0,1:T(8,128)} fusion(f32[1024,1024]{1,0:T(8,128)} %param.4), kind=kOutput, calls=%fused_computation.235 | convolution fusion | flops 12884901888 | bytes 8388608 | tf_op jit(solution)/shard_map/dot_general | solution.py:22
  26.3 142.7 %all-reduce.3.cloned.1.call-done = f32[1024,1024]{0,1:T(8,128)} async-done(((f32[1024,1024]{0,1:T(8,128)}), f32[1024,1024]{0,1:T(8,128)}) %all-reduce.3.cloned.1.call-update) | async-done | bytes 4194320 | tf_op jit(solution)/shard_map/psum | solution.py:25
  169.0 5.0 select_add_fusion
  174.0 5.5 copy.77
  179.5 4.5 fusion.2
  184.0 1.9 copy-done.2
  185.9 11.7 %cholesky.222 = f32[128,128]{1,0:T(8,128)S(1)} custom-call(f32[128,128]{1,0:T(8,128)S(1)} %cholesky.577), custom_call_target="Cholesky" | custom-call | tf_op jit(solution)/shard_map/jit(cholesky)/cholesky | solution.py:29
  197.8 9.8 %custom-call.64 = f32[1,128,128]{1,2,0:T(8,128)S(1)} custom-call(f32[1,128,128]{2,1,0:T(8,128)S(1)} %get-tuple-element.52), custom_call_target="InvertDiagBlocksLowerTriangular" | custom-call | tf_op jit(solution)/shard_map/jit(cholesky)/cholesky | solution.py:29
  207.6 1.5 fusion.15
  209.3 1.6 convolution_subtract_fusion
  210.9 11.7 %cholesky.243 = f32[128,128]{1,0:T(8,128)S(1)} custom-call(f32[128,128]{1,0:T(8,128)S(1)} %cholesky.581), custom_call_target="Cholesky" | custom-call | tf_op jit(solution)/shard_map/jit(cholesky)/cholesky | solution.py:29
  223.0 9.8 %custom-call.65 = f32[1,128,128]{1,2,0:T(8,128)S(1)} custom-call(f32[1,128,128]{2,1,0:T(8,128)S(1)} %get-tuple-element.50), custom_call_target="InvertDiagBlocksLowerTriangular" | custom-call | tf_op jit(solution)/shard_map/jit(cholesky)/cholesky | solution.py:29
  233.9 2.0 copy-done.1
  235.8 2.4 convolution_subtract_fusion.1
  238.3 11.7 %cholesky.466 = f32[128,128]{1,0:T(8,128)S(1)} custom-call(f32[128,128]{1,0:T(8,128)S(1)} %cholesky.586), custom_call_target="Cholesky" | custom-call | tf_op jit(solution)/shard_map/jit(cholesky)/cholesky | solution.py:29
  250.8 9.8 %custom-call.66 = f32[1,128,128]{1,2,0:T(8,128)S(1)} custom-call(f32[1,128,128]{2,1,0:T(8,128)S(1)} %get-tuple-element.48), custom_call_target="InvertDiagBlocksLowerTriangular" | custom-call | tf_op jit(solution)/shard_map/jit(cholesky)/cholesky | solution.py:29
  261.8 3.6 convolution_subtract_fusion.2
  265.4 11.7 %cholesky.485 = f32[128,128]{1,0:T(8,128)S(1)} custom-call(f32[128,128]{1,0:T(8,128)S(1)} %cholesky.591), custom_call_target="Cholesky" | custom-call | tf_op jit(solution)/shard_map/jit(cholesky)/cholesky | solution.py:29
  277.9 9.8 %custom-call.67 = f32[1,128,128]{1,2,0:T(8,128)S(1)} custom-call(f32[1,128,128]{2,1,0:T(8,128)S(1)} %get-tuple-element.46), custom_call_target="InvertDiagBlocksLowerTriangular" | custom-call | tf_op jit(solution)/shard_map/jit(cholesky)/cholesky | solution.py:29
  288.8 3.2 convolution_subtract_fusion.3
  292.0 11.9 %cholesky.504 = f32[128,128]{1,0:T(8,128)S(1)} custom-call(f32[128,128]{1,0:T(8,128)S(1)} %cholesky.596), custom_call_target="Cholesky" | custom-call | tf_op jit(solution)/shard_map/jit(cholesky)/cholesky | solution.py:29
  304.7 9.8 %custom-call.68 = f32[1,128,128]{1,2,0:T(8,128)S(1)} custom-call(f32[1,128,128]{2,1,0:T(8,128)S(1)} %get-tuple-element.44), custom_call_target="InvertDiagBlocksLowerTriangular" | custom-call | tf_op jit(solution)/shard_map/jit(cholesky)/cholesky | solution.py:29
  315.6 3.1 convolution_subtract_fusion.4
  318.7 11.7 %cholesky.524 = f32[128,128]{1,0:T(8,128)S(1)} custom-call(f32[128,128]{1,0:T(8,128)S(1)} %cholesky.601), custom_call_target="Cholesky" | custom-call | tf_op jit(solution)/shard_map/jit(cholesky)/cholesky | solution.py:29
  331.2 9.8 %custom-call.69 = f32[1,128,128]{1,2,0:T(8,128)S(1)} custom-call(f32[1,128,128]{2,1,0:T(8,128)S(1)} %get-tuple-element.42), custom_call_target="InvertDiagBlocksLowerTriangular" | custom-call | tf_op jit(solution)/shard_map/jit(cholesky)/cholesky | solution.py:29
  342.0 2.9 convolution_subtract_fusion.5
  344.9 11.7 %cholesky.544 = f32[128,128]{1,0:T(8,128)S(1)} custom-call(f32[128,128]{1,0:T(8,128)S(1)} %cholesky.606), custom_call_target="Cholesky" | custom-call | tf_op jit(solution)/shard_map/jit(cholesky)/cholesky | solution.py:29
  357.4 9.8 %custom-call.70 = f32[1,128,128]{1,2,0:T(8,128)S(1)} custom-call(f32[1,128,128]{2,1,0:T(8,128)S(1)} %get-tuple-element.40), custom_call_target="InvertDiagBlocksLowerTriangular" | custom-call | tf_op jit(solution)/shard_map/jit(cholesky)/cholesky | solution.py:29
  368.1 2.1 convolution_subtract_fusion.6
  370.2 11.7 %cholesky.562 = f32[128,128]{1,0:T(8,128)S(1)} custom-call(f32[128,128]{1,0:T(8,128)S(1)} %convolution_subtract_fusion.6), custom_call_target="Cholesky" | custom-call | tf_op jit(solution)/shard_map/jit(cholesky)/cholesky | solution.py:29
  392.4 4.9 select_select_fusion
  397.3 23.7 %while.1 = (s32[]{:T(128)}, f32[1024,1024]{0,1:T(8,128)}, s32[8,2]{0,1:T(2,128)S(1)}, f32[8,128,128]{2,1,0:T(8,128)S(1)}, s32[]{:T(128)}) while((s32[]{:T(128)}, f32[1024,1024]{0,1:T(8,128)}, s32[8,2]{0,1:T(2,128)S(1)}, f32[8,128,128]{2,1,0:T(8,128)S(1)}, s32[]{:T(128)}) %tuple.52), condition=%wide.while_cond, body=%wide.while_body.sunk | while | flops 2 | bytes 393329 | solution.py:11
  397.9 2.2 dynamic-slice.7
  400.9 2.2 dynamic-slice.7
  403.9 2.2 dynamic-slice.7
  406.8 2.2 dynamic-slice.7
  409.8 2.2 dynamic-slice.7
  412.8 2.2 dynamic-slice.7
  415.8 2.2 dynamic-slice.7
  418.7 2.2 dynamic-slice.7
  421.0 78.8 %custom-call.71 = f32[8,128,128]{1,2,0:T(8,128)S(1)} custom-call(f32[8,128,128]{2,1,0:T(8,128)S(1)} %get-tuple-element.12), custom_call_target="InvertDiagBlocksLowerTriangular" | custom-call | tf_op jit(solution)/shard_map/triangular_solve | solution.py:11
  508.2 1.4 convolution_subtract_fusion.18
  515.7 1.4 convolution_subtract_fusion.17
  517.3 1.4 convolution_subtract_fusion.16
  519.0 1.5 convolution_subtract_fusion.15
  521.3 11.9 %all_to_all.5 = f32[8,8,1024]{2,1,0:T(8,128)S(1)} all-to-all(f32[8,8,1024]{2,1,0:T(8,128)S(1)} %copy.95), channel_id=1, replica_groups=mesh['dp'=8,'group'=4] {'dp'}, dimensions={0} | all-to-all | bytes 524288 | tf_op jit(solution)/shard_map/all_to_all | solution.py:44
  534.2 14.9 %all-gather.2.cloned.1.call-done = f32[8,32,1024]{2,0,1:T(8,128)} async-done(((f32[8,8,1024]{2,0,1:T(8,128)}), f32[8,32,1024]{2,0,1:T(8,128)}) %all-gather.2.cloned.1.call-update) | async-done | bytes 1048592 | tf_op jit(solution)/shard_map/all_gather | solution.py:48
  549.1 6.9 %fusion.3 = f32[8,32,1024]{2,1,0:T(8,128)S(1)} fusion(f32[1024,1024]{1,0:T(8,128)} %param.4, f32[8,32,1024]{2,0,1:T(8,128)} %all-gather.2.cloned.1.call-done), kind=kOutput, calls=%fused_computation.11 | convolution fusion | flops 3221487616 | bytes 6291456 | tf_op jit(solution)/shard_map/dot_general | solution.py:46
  (152 shorter events, 41.9 us)
Async XLA Ops:
  6.5 18.8 %copy-start = (s32[8,8]{1,0:T(8,128)S(1)}, s32[8,8]{1,0:T(8,128)}, u32[]{:S(2)}) copy-start(s32[8,8]{1,0:T(8,128)} %param.6) | copy-start | bytes 772
  6.5 162.5 %all-reduce.3.cloned.1.call-start = ((), (), s32[]{:S(2)}) async-start(), calls=%async_computation.1 | async-start | bytes 8388608 | tf_op jit(solution)/shard_map/psum | solution.py:25
  24.4 0.7 copy-start.4
  24.4 524.7 %all-gather.2.cloned.1.call-start = ((), (), s32[]{:S(2)}) async-start(), calls=%async_computation.2 | async-start | bytes 1310720 | tf_op jit(solution)/shard_map/all_gather | solution.py:48
  184.0 1.9 copy-start.2
  233.9 2.0 copy-start.1
  392.4 107.5 %copy-start.3 = (f32[2,8,1024]{2,1,0:T(8,128)S(1)}, f32[2,8,1024]{2,1,0:T(8,128)}, u32[]{:S(2)}) copy-start(f32[2,8,1024]{2,1,0:T(8,128)} %param.5) | copy-start | bytes 196612
Sparse Core Ops, SparseCore 0:
  24.5 144.4 all-reduce.2
  534.3 14.7 all-gather.1
where the time goes:
time: 572 us; the launch traced here: 565 us
  other arithmetic  261 us (46%)
  waiting for transfers between devices  158 us (28%)
  matrix products  71.8 us (13%)
  local copies, waits for them, and re-layouts  42.2 us (7%)
  between operations  19.4 us (3%)
  blocking collectives  11.9 us (2%)
    another operation x30, other arithmetic, local(): factor = jnp.linalg.cholesky(gram_matrix)  167 us
    psum x1, waiting for transfers between devices, local(): summed = lax.psum(partial_gram, ('dp', 'group'))  143 us
    another operation x3, other arithmetic, cholesky_apply(): lax.linalg.triangular_solve(factor, middle, left_side=True, lower=True, t...  83.7 us
    another operation x14, matrix products, local(): factor = jnp.linalg.cholesky(gram_matrix)  26.2 us
    another operation x40, local copies, waits for them, and re-layouts  23.5 us
    dot_general x1, matrix products, local(): lax.dot_general(train_grads, train_grads, (((0,), (0,)), ((), ())), preci...  17.8 us
    all_gather x1, waiting for transfers between devices, local(): lax.all_gather(arrived, 'group', axis=1, tiled=True)  14.9 us
    all_to_all x1, blocking collectives, local(): lax.all_to_all(outgoing, 'dp', split_axis=0, concat_axis=0, tiled=True)  11.9 us
  transfers between devices with their start and end apart: 2, of which 2 were waited for; matrix products, arithmetic and copies ran while one was open for 0% of the time, Pallas kernels for 0%

commit v1 on v0

v1 whole, which is shorter than its diff:
```python
import functools

import jax
import jax.numpy as jnp
from jax import lax
from jax.experimental import pallas as pl
from jax.experimental.pallas import tpu as pltpu
from jax.sharding import PartitionSpec as P

damping = 0.1
BLOCK = 128
SUB = 8
highest = lax.Precision.HIGHEST


def invert_block(rows):
    rows = list(rows)
    lane = lax.broadcasted_iota(jnp.int32, (SUB, BLOCK), 1)
    sub = lax.broadcasted_iota(jnp.int32, (SUB, BLOCK), 0)
    is_row = [sub == j for j in range(SUB)]
    for p in range(BLOCK // SUB):
        base = p * SUB
        panel = rows[p]
        cols = [jnp.broadcast_to(panel[:, base + j : base + j + 1], (SUB, BLOCK)) for j in range(SUB)]
        inside = (lane >= base) & (lane < base + SUB)
        new = jnp.where(inside, jnp.where(lane - base == sub, 1.0, 0.0), panel)
        for j in range(SUB):
            inv = 1.0 / cols[j][j : j + 1, :]
            factor = jnp.where(is_row[j], 0.0, cols[j])
            pivot = new[j : j + 1, :] * inv
            for l in range(j + 1, SUB):
                head = cols[l][j : j + 1, :] * inv
                cols[l] = jnp.where(is_row[j], head, cols[l]) - factor * head
            new = jnp.where(is_row[j], pivot, new) - factor * pivot
        for r in range(BLOCK // SUB):
            if r == p:
                continue
            old = rows[r]
            total = jnp.where(inside, 0.0, old)
            for j in range(SUB):
                total = total - old[:, base + j : base + j + 1] * new[j : j + 1, :]
            rows[r] = total
        rows[p] = new
    return rows


def dot(a, b, dims):
    return lax.dot_general(a, b, (dims, ((), ())), precision=highest, preferred_element_type=jnp.float32)


def solve_kernel(rows_total, request, gram, blocks, out, work, upper, diag):
    features = gram.shape[0]
    steps = features // BLOCK
    slots = request.shape[0]
    vb = blocks.shape[1]
    scale = features ** (-0.5)
    for i in range(steps):
        at = pl.ds(i * BLOCK, BLOCK)
        row = lax.broadcasted_iota(jnp.int32, (BLOCK, features), 0) + i * BLOCK
        col = lax.broadcasted_iota(jnp.int32, (BLOCK, features), 1)
        work[at, :] = gram[at, :] / rows_total + jnp.where(row == col, damping, 0.0)

    def pick(j, carry):
        w = request[j]
        live = jnp.where(w >= 0, scale, 0.0).astype(jnp.float32)
        out[pl.ds(pl.multiple_of(j * vb, vb), vb), :] = blocks[jnp.maximum(w, 0)] * live
        return carry

    lax.fori_loop(0, slots, pick, 0)

    def forward(k, carry):
        at = pl.ds(pl.multiple_of(k * BLOCK, BLOCK), BLOCK)
        block = work[at, at]
        inverse = jnp.concatenate(invert_block([block[SUB * r : SUB * r + SUB] for r in range(BLOCK // SUB)]), axis=0)
        diag[at, :] = inverse
        col = lax.broadcasted_iota(jnp.int32, (BLOCK, features), 1)
        panel = jnp.where(col >= (k + 1) * BLOCK, work[at, :], 0.0)
        scaled = dot(inverse, panel, ((1,), (0,)))
        upper[at, :] = scaled
        out[...] -= dot(out[:, at], scaled, ((1,), (0,)))

        def trail(i, carry):
            to = pl.ds(pl.multiple_of(i * BLOCK, BLOCK), BLOCK)
            work[to, :] -= dot(work[at, to], upper[at, :], ((0,), (0,)))
            return carry

        lax.fori_loop(k + 1, steps, trail, 0)
        return carry

    lax.fori_loop(0, steps, forward, 0)

    def backward(i, carry):
        k = steps - 1 - i
        at = pl.ds(pl.multiple_of(k * BLOCK, BLOCK), BLOCK)
        out[:, at] = dot(out[:, at], diag[at, :], ((1,), (0,))) - dot(out[...], upper[at, :], ((1,), (1,)))
        return carry

    lax.fori_loop(0, steps, backward, 0)


def solve(gram_sum, blocks, request, rows_total):
    features = gram_sum.shape[0]
    slots, vb = request.shape[0], blocks.shape[1]
    return pl.pallas_call(
        functools.partial(solve_kernel, rows_total),
        out_shape=jax.ShapeDtypeStruct((slots * vb, features), jnp.float32),
        in_specs=[
            pl.BlockSpec(memory_space=pltpu.SMEM),
            pl.BlockSpec(memory_space=pltpu.VMEM),
            pl.BlockSpec(memory_space=pltpu.VMEM),
        ],
        out_specs=pl.BlockSpec(memory_space=pltpu.VMEM),
        scratch_shapes=[
            pltpu.VMEM((features, features), jnp.float32),
            pltpu.VMEM((features, features), jnp.float32),
            pltpu.VMEM((features, BLOCK), jnp.float32),
        ],
        compiler_params=pltpu.CompilerParams(vmem_limit_bytes=56 * 2**20),
        cost_estimate=pl.CostEstimate(flops=10**10, bytes_accessed=10**7, transcendentals=0),
    )(request, gram_sum, blocks)


def local(train_grads, val_grads, wanted, owner):
    features = train_grads.shape[1]
    devices, group = lax.axis_size("dp"), lax.axis_size("group")
    rows_total = train_grads.shape[0] * devices * group
    gathered = lax.all_gather(val_grads, ("dp", "group"), axis=0, tiled=False)
    per, part = val_grads.shape[0], val_grads.shape[1]
    blocks = gathered.reshape(devices, group, per, part, features).transpose(0, 2, 1, 3, 4)
    blocks = blocks.reshape(devices * per, group * part, features)
    own_index = lax.axis_index("dp")
    mine = jnp.sum(jnp.where(owner == own_index, jnp.arange(devices, dtype=jnp.int32), 0))
    request = lax.dynamic_index_in_dim(wanted, mine, 0, keepdims=False)
    partial_gram = lax.dot_general(train_grads, train_grads, (((0,), (0,)), ((), ())), precision=highest)
    summed = lax.psum(partial_gram, ("dp", "group"))
    solved = solve(summed, blocks, request, rows_total)
    return lax.dot_general(train_grads, solved, (((1,), (1,)), ((), ())), precision=highest)


def solution(mesh):
    in_specs = (P(("dp", "group"), None), P("dp", "group", None), P(), P())
    out_specs = P(("dp", "group"), None)
    return jax.shard_map(local, mesh=mesh, in_specs=in_specs, out_specs=out_specs, check_vma=False)
```

time: 572 us -> 309 us (0.54); the launches traced: 565 us -> 308 us
  other arithmetic: 261 us -> 0.63 us
  Pallas kernels: 0 us -> 79.8 us
  matrix products: 71.8 us -> 22.6 us
  local copies, waits for them, and re-layouts: 42.2 us -> 5.65 us
  waiting for transfers between devices: 158 us -> 184 us
  blocking collectives: 11.9 us -> 0 us
    another operation x33 -> x0, other arithmetic: 251 us -> none  [the longest x30 167 us: local(): factor = jnp.linalg.cholesky(gram_matrix)]
    pallas_call x0 -> x1, Pallas kernels: none -> 79.8 us  [solve(): pl.pallas_call(functools.partial(solve_kernel, rows_total), out_shape=jax...]
    another operation x44 -> x0, matrix products: 46.7 us -> none  [the longest x14 26.2 us: local(): factor = jnp.linalg.cholesky(gram_matrix)]
    another operation x70 -> x0, local copies, waits for them, and re-layouts: 29.1 us -> none
    all_gather x1, waiting for transfers between devices: 14.9 us -> 40.6 us  [local(): gathered = lax.all_gather(val_grads, ('dp', 'group'), axis=0, tiled=False)]
    all_to_all x1 -> x0, blocking collectives: 11.9 us -> none  [local(): lax.all_to_all(outgoing, 'dp', split_axis=0, concat_axis=0, tiled=True)]
  transfers between devices with their start and end apart: 2 -> 2, of which waited for: 2 -> 2; matrix products, arithmetic and copies ran while one was open for 0% -> 7% of each run, Pallas kernels for 0% -> 0%
where the time goes in v1:
time: 309 us; the launch traced here: 308 us
  waiting for transfers between devices  184 us (60%)
  Pallas kernels  79.8 us (26%)
  matrix products  22.6 us (7%)
  between operations  15.4 us (5%)
  local copies, waits for them, and re-layouts  5.65 us (2%)
    psum x1, waiting for transfers between devices, local(): summed = lax.psum(partial_gram, ('dp', 'group'))  143 us
    pallas_call x1, Pallas kernels, solve(): pl.pallas_call(functools.partial(solve_kernel, rows_total), out_shape=jax...  79.8 us
    all_gather x1, waiting for transfers between devices, local(): gathered = lax.all_gather(val_grads, ('dp', 'group'), axis=0, tiled=False)  40.6 us
    dot_general x1, matrix products, local(): lax.dot_general(train_grads, train_grads, (((0,), (0,)), ((), ())), preci...  17.6 us
  transfers between devices with their start and end apart: 2, of which 2 were waited for; matrix products, arithmetic and copies ran while one was open for 7% of the time, Pallas kernels for 0%

profile of v1, /device:TPU:0, one launch (start us, length us, event | category | flops | bytes accessed | tf_op | source)
XLA Modules:
  0.0 308.4 jit_solution(4233016031930025456)
XLA Ops:
  6.5 0.0 copy-start
  6.5 0.0 all-gather.3.cloned.1.call-start
  6.5 0.7 all-gather.3.cloned.1.call-update
  7.3 0.0 all-reduce.2.cloned.1.call-start
  7.3 17.6 %fusion.1 = f32[1024,1024]{1,0:T(8,128)} fusion(f32[1024,1024]{1,0:T(8,128)} %param.4), kind=kOutput, calls=%fused_computation.4 | convolution fusion | flops 12884901888 | bytes 8388608 | tf_op jit(solution)/shard_map/dot_general | solution.py:134
  24.9 0.0 copy-start.2
  24.9 0.0 all-reduce.2.cloned.1.call-update
  25.0 0.6 copy-done.2
  25.6 0.6 fusion
  28.2 0.0 copy-done
  28.2 0.6 dynamic-slice_bitcast_fusion.request
  28.7 40.6 %all-gather.3.cloned.1.call-done = f32[64,8,1024]{2,1,0:T(8,128)} async-done(((f32[2,8,1024]{2,1,0:T(8,128)}), f32[64,8,1024]{2,1,0:T(8,128)}) %all-gather.3.cloned.1.call-update) | async-done | bytes 2097168 | tf_op jit(solution)/shard_map/all_gather | solution.py:127
  69.4 3.2 %copy.7 = f32[8,4,2,8,1024]{4,3,1,2,0:T(8,128)} copy(f32[8,4,2,8,1024]{4,3,2,1,0:T(8,128)} %bitcast.12) | data formatting | bytes 4194304 | tf_op jit(solution)/shard_map/reshape | solution.py:129
  72.5 143.0 %all-reduce.2.cloned.1.call-done.gram = f32[1024,1024]{1,0:T(8,128)} async-done(((f32[1024,1024]{1,0:T(8,128)}), f32[1024,1024]{1,0:T(8,128)}) %all-reduce.2.cloned.1.call-update) | async-done | bytes 4194320 | tf_op jit(solution)/shard_map/psum | solution.py:135
  215.5 0.0 copy-start.1
  215.5 79.8 %shard_map.46 = f32[256,1024]{1,0:T(8,128)} custom-call(s32[8]{0:T(128)} %dynamic-slice_bitcast_fusion.request, f32[1024,1024]{1,0:T(8,128)} %all-reduce.2.cloned.1.call-done.gram, f32[16,32,1024]{2,1,0:T(8,128)} %bitcast.13), custom_call_target="tpu_custom_call" | custom-call | flops 10000000000 | bytes 10000000 | tf_op jit(solution)/shard_map/pallas_call | solution.py:104
  295.3 0.0 copy-done.1
  295.3 5.0 %convolution_bitcast_fusion = f32[1024,256]{0,1:T(8,128)S(1)} fusion(f32[256,1024]{1,0:T(8,128)} %shard_map.46, f32[1024,1024]{1,0:T(8,128)S(1)} %copy-done.1), kind=kOutput, calls=%fused_computation | convolution fusion | flops 3221225472 | bytes 6291456 | tf_op jit(solution)/shard_map/dot_general | solution.py:137
  300.3 1.3 copy.8
Async XLA Ops:
  6.5 21.6 %copy-start = (s32[8,8]{1,0:T(8,128)S(1)}, s32[8,8]{1,0:T(8,128)}, u32[]{:S(2)}) copy-start(s32[8,8]{1,0:T(8,128)} %param.6) | copy-start | bytes 772
  6.5 62.8 %all-gather.3.cloned.1.call-start = ((), (), s32[]{:S(2)}) async-start(), calls=%async_computation.1 | async-start | bytes 2162688 | tf_op jit(solution)/shard_map/all_gather | solution.py:127
  7.3 208.3 %all-reduce.2.cloned.1.call-start = ((), (), s32[]{:S(2)}) async-start(), calls=%async_computation | async-start | bytes 8388608 | tf_op jit(solution)/shard_map/psum | solution.py:135
  24.9 0.7 copy-start.2
  215.5 79.8 %copy-start.1 = (f32[1024,1024]{1,0:T(8,128)S(1)}, f32[1024,1024]{1,0:T(8,128)}, u32[]{:S(2)}) copy-start(f32[1024,1024]{1,0:T(8,128)} %param.4) | copy-start | bytes 12582916
Sparse Core Ops, SparseCore 0:
  10.2 59.1 all-gather.2
  74.9 140.5 all-reduce.1

commit v2 on v1

v2 whole, which is shorter than its diff:
```python
import functools

import jax
import jax.numpy as jnp
from jax import lax
from jax.experimental import pallas as pl
from jax.experimental.pallas import tpu as pltpu
from jax.sharding import PartitionSpec as P

damping = 0.1
BLOCK = 128
SUB = 8
STREAMS = 3
MESH = pl.DeviceIdType.MESH


def upper_blocks(features):
    steps = features // BLOCK
    return [(i, j) for i in range(steps) for j in range(i, steps)]


def sum_plan(dp, group, features):
    rows = len(upper_blocks(features)) * BLOCK
    bits = [("group", 1 << b) for b in range(group.bit_length() - 1)]
    bits += [("dp", 1 << b) for b in range(dp.bit_length() - 1)]
    if (1 << len(bits)) != dp * group or group < 2 or dp < 2:
        return None
    if rows % (STREAMS * SUB * dp * group):
        return None
    first, rest = bits[0], bits[1:]
    turning, last = rest[:-1], rest[-1:]
    count = len(turning)
    streams = [[first] + [turning[(s + t) % count] for t in range(count)] + last for s in range(STREAMS)]
    return streams


def place_of(bit):
    axis, weight = bit
    index = lax.axis_index(axis)
    mine = lax.rem(index // weight, 2)
    return mine, {axis: index + weight * (1 - 2 * mine)}


def sum_kernel(streams, gram, out, total, landed, send_sem, recv_sem):
    features = gram.shape[0]
    rows = total.shape[0]
    depth = len(streams[0])
    bits = sorted(set(streams[0]))
    barrier = pltpu.get_barrier_semaphore()
    for bit in bits:
        pl.semaphore_signal(barrier, inc=1, device_id=place_of(bit)[1], device_id_type=MESH)
    for n, (i, j) in enumerate(upper_blocks(features)):
        total[n * BLOCK : (n + 1) * BLOCK, :] = gram[i * BLOCK : (i + 1) * BLOCK, j * BLOCK : (j + 1) * BLOCK]
    pl.semaphore_wait(barrier, len(bits))

    half = rows // 2
    share = half // STREAMS
    core, sibling = place_of(streams[0][0])

    def at(offset, size):
        return pl.ds(pl.multiple_of(offset, SUB), size)

    held = [[None] * depth for _ in streams]
    away = [[None] * depth for _ in streams]
    slot = [[None] * depth for _ in streams]
    free = 0
    for s, order in enumerate(streams):
        offset, size = core * half + s * share, share
        held[s][0] = (offset, size)
        away[s][0] = ((1 - core) * half + s * share, size)
        for t in range(1, depth):
            mine, _ = place_of(order[t])
            size = size // 2
            away[s][t] = (offset + (1 - mine) * size, size)
            offset = offset + mine * size
            held[s][t] = (offset, size)
        for t in range(depth):
            slot[s][t] = (free, held[s][t][1])
            free += held[s][t][1]

    def out_copy(s, t):
        return pltpu.make_async_remote_copy(
            src_ref=total.at[at(*away[s][t])],
            dst_ref=landed.at[pl.ds(*slot[s][t])],
            send_sem=send_sem.at[0, s, t],
            recv_sem=recv_sem.at[0, s, t],
            device_id=place_of(streams[s][t])[1],
            device_id_type=MESH,
        )

    def back_copy(s, t):
        return pltpu.make_async_remote_copy(
            src_ref=out.at[at(*held[s][t])],
            dst_ref=out.at[at(*held[s][t])],
            send_sem=send_sem.at[1, s, t],
            recv_sem=recv_sem.at[1, s, t],
            device_id=place_of(streams[s][t])[1],
            device_id_type=MESH,
        )

    outs = [[out_copy(s, t) for t in range(depth)] for s in range(len(streams))]
    backs = [[back_copy(s, t) for t in range(depth)] for s in range(len(streams))]
    for s in range(len(streams)):
        outs[s][0].start()
    for t in range(depth):
        for s in range(len(streams)):
            outs[s][t].wait()
            here = at(*held[s][t])
            if t + 1 < depth:
                total[here, :] += landed[pl.ds(*slot[s][t]), :]
                outs[s][t + 1].start()
            else:
                out[here, :] = total[here, :] + landed[pl.ds(*slot[s][t]), :]
                backs[s][t].start()
    for t in reversed(range(depth)):
        for s in range(len(streams)):
            backs[s][t].wait()
            if t > 0:
                backs[s][t - 1].start()


def sum_gram(partial_gram, streams):
    features = partial_gram.shape[0]
    rows = len(upper_blocks(features)) * BLOCK
    depth = len(streams[0])
    return pl.pallas_call(
        functools.partial(sum_kernel, streams),
        out_shape=jax.ShapeDtypeStruct((rows, BLOCK), jnp.float32),
        in_specs=[pl.BlockSpec(memory_space=pltpu.VMEM)],
        out_specs=pl.BlockSpec(memory_space=pltpu.VMEM),
        scratch_shapes=[
            pltpu.VMEM((rows, BLOCK), jnp.float32),
            pltpu.VMEM((rows, BLOCK), jnp.float32),
            pltpu.SemaphoreType.DMA((2, STREAMS, depth)),
            pltpu.SemaphoreType.DMA((2, STREAMS, depth)),
        ],
        compiler_params=pltpu.CompilerParams(
            collective_id=0, has_side_effects=True, vmem_limit_bytes=24 * 2**20
        ),
        cost_estimate=pl.CostEstimate(flops=10**10, bytes_accessed=10**8, transcendentals=0),
    )(partial_gram)


def invert_block(rows):
    rows = list(rows)
    lane = lax.broadcasted_iota(jnp.int32, (SUB, BLOCK), 1)
    sub = lax.broadcasted_iota(jnp.int32, (SUB, BLOCK), 0)
    is_row = [sub == j for j in range(SUB)]
    for p in range(BLOCK // SUB):
        base = p * SUB
        panel = rows[p]
        cols = [jnp.broadcast_to(panel[:, base + j : base + j + 1], (SUB, BLOCK)) for j in range(SUB)]
        inside = (lane >= base) & (lane < base + SUB)
        new = jnp.where(inside, jnp.where(lane - base == sub, 1.0, 0.0), panel)
        for j in range(SUB):
            inv = 1.0 / cols[j][j : j + 1, :]
            factor = jnp.where(is_row[j], 0.0, cols[j])
            pivot = new[j : j + 1, :] * inv
            for l in range(j + 1, SUB):
                head = cols[l][j : j + 1, :] * inv
                cols[l] = jnp.where(is_row[j], head, cols[l]) - factor * head
            new = jnp.where(is_row[j], pivot, new) - factor * pivot
        for r in range(BLOCK // SUB):
            if r == p:
                continue
            old = rows[r]
            total = jnp.where(inside, 0.0, old)
            for j in range(SUB):
                total = total - old[:, base + j : base + j + 1] * new[j : j + 1, :]
            rows[r] = total
        rows[p] = new
    return rows


def halves(x):
    high = x.astype(jnp.bfloat16)
    return high, (x - high.astype(jnp.float32)).astype(jnp.bfloat16)


def dot(a, b):
    a_high, a_low = halves(a)
    b_high, b_low = halves(b)
    left = jnp.concatenate([a_high, a_high, a_low], axis=1)
    right = jnp.concatenate([b_high, b_low, b_high], axis=0)
    return jnp.dot(left, right, preferred_element_type=jnp.float32)


def solve_kernel(rows_total, chunk, request, gram, blocks, out, work, scaled, right):
    features = out.shape[1]
    steps = features // BLOCK
    slots = request.shape[0]
    part = blocks.shape[3]
    vb = blocks.shape[1] * part
    scale = features ** (-0.5)
    diagonal = lax.broadcasted_iota(jnp.int32, (BLOCK, BLOCK), 0) == lax.broadcasted_iota(jnp.int32, (BLOCK, BLOCK), 1)
    for n, (i, j) in enumerate(upper_blocks(features)):
        block = gram[n * BLOCK : (n + 1) * BLOCK, :] / rows_total
        if i == j:
            block = block + jnp.where(diagonal, damping, 0.0)
        else:
            work[j * BLOCK : (j + 1) * BLOCK, i * BLOCK : (i + 1) * BLOCK] = block.T
        work[i * BLOCK : (i + 1) * BLOCK, j * BLOCK : (j + 1) * BLOCK] = block

    def pick(j, carry):
        w = request[j]
        live = jnp.where(w >= 0, scale, 0.0).astype(jnp.float32)
        known = jnp.maximum(w, 0)
        holder, inner = lax.div(known, blocks.shape[2]), lax.rem(known, blocks.shape[2])
        for g in range(blocks.shape[1]):
            to = pl.ds(pl.multiple_of(features + j * vb + g * part, part), part)
            work[to, :] = blocks[holder, g, inner] * live
        return carry

    lax.fori_loop(0, slots, pick, 0)

    def step(k, carry):
        at = pl.ds(pl.multiple_of(k * BLOCK, BLOCK), BLOCK)
        block = work[at, at]
        inverse = jnp.concatenate(invert_block([block[SUB * r : SUB * r + SUB] for r in range(BLOCK // SUB)]), axis=0)
        scaled[...] = inverse
        col = lax.broadcasted_iota(jnp.int32, (BLOCK, features), 1)
        outside = (col < k * BLOCK) | (col >= (k + 1) * BLOCK)
        high, low = halves(jnp.where(outside, work[at, :], 0.0))
        right[0:BLOCK, :] = high
        right[BLOCK : 2 * BLOCK, :] = low
        right[2 * BLOCK :, :] = high

        def update(i, carry):
            to = pl.ds(pl.multiple_of(i * chunk, chunk), chunk)
            column = dot(work[to, at], scaled[...])
            column_high, column_low = halves(column)
            left = jnp.concatenate([column_high, column_high, column_low], axis=1)
            work[to, :] -= jnp.dot(left, right[...], preferred_element_type=jnp.float32)
            work[to, at] = column
            return carry

        lax.fori_loop((k + 1) * BLOCK // chunk, work.shape[0] // chunk, update, 0)
        return carry

    lax.fori_loop(0, steps, step, 0)
    out[...] = work[features:, :]


def solve(gram_sum, blocks, request, rows_total):
    features = blocks.shape[4]
    slots, vb = request.shape[0], blocks.shape[1] * blocks.shape[3]
    chunk = 2 * BLOCK
    return pl.pallas_call(
        functools.partial(solve_kernel, rows_total, chunk),
        out_shape=jax.ShapeDtypeStruct((slots * vb, features), jnp.float32),
        in_specs=[
            pl.BlockSpec(memory_space=pltpu.SMEM),
            pl.BlockSpec(memory_space=pltpu.VMEM),
            pl.BlockSpec(memory_space=pltpu.VMEM),
        ],
        out_specs=pl.BlockSpec(memory_space=pltpu.VMEM),
        scratch_shapes=[
            pltpu.VMEM((features + slots * vb, features), jnp.float32),
            pltpu.VMEM((BLOCK, BLOCK), jnp.float32),
            pltpu.VMEM((3 * BLOCK, features), jnp.bfloat16),
        ],
        compiler_params=pltpu.CompilerParams(vmem_limit_bytes=56 * 2**20),
        cost_estimate=pl.CostEstimate(flops=10**10, bytes_accessed=10**7, transcendentals=0),
    )(request, gram_sum, blocks)


def local(streams, train_grads, val_grads, wanted, owner):
    features = train_grads.shape[1]
    devices, group = lax.axis_size("dp"), lax.axis_size("group")
    rows_total = train_grads.shape[0] * devices * group
    gathered = lax.all_gather(val_grads, ("dp", "group"), axis=0, tiled=False)
    blocks = gathered.reshape((devices, group) + val_grads.shape)
    own_index = lax.axis_index("dp")
    mine = jnp.sum(jnp.where(owner == own_index, jnp.arange(devices, dtype=jnp.int32), 0))
    request = lax.dynamic_index_in_dim(wanted, mine, 0, keepdims=False)
    partial_gram = lax.dot_general(
        train_grads, train_grads, (((0,), (0,)), ((), ())), precision=lax.Precision.HIGH
    )
    if streams is None:
        summed = lax.psum(partial_gram, ("dp", "group"))
        summed = jnp.concatenate(
            [summed[i * BLOCK : (i + 1) * BLOCK, j * BLOCK : (j + 1) * BLOCK] for i, j in upper_blocks(features)]
        )
    else:
        summed = sum_gram(partial_gram, streams)
    solved = solve(summed, blocks, request, rows_total)
    return lax.dot_general(train_grads, solved, (((1,), (1,)), ((), ())), precision=lax.Precision.HIGH)


def solution(mesh):
    in_specs = (P(("dp", "group"), None), P("dp", "group", None), P(), P())
    out_specs = P(("dp", "group"), None)

    def whole(train_grads, val_grads, wanted, owner):
        streams = sum_plan(mesh.shape["dp"], mesh.shape["group"], train_grads.shape[1])
        return jax.shard_map(
            functools.partial(local, streams), mesh=mesh, in_specs=in_specs, out_specs=out_specs, check_vma=False
        )(train_grads, val_grads, wanted, owner)

    return whole
```

time: 309 us -> 134 us (0.43)
  waiting for transfers between devices: 184 us -> 1.09 us
  Pallas kernels: 79.8 us -> 98.9 us
  matrix products: 22.6 us -> 13.7 us
    psum x1 -> x0, waiting for transfers between devices: 143 us -> none  [local(): summed = lax.psum(partial_gram, ('dp', 'group'))]
    all_gather x1, waiting for transfers between devices: 40.6 us -> 0.38 us  [local(): gathered = lax.all_gather(val_grads, ('dp', 'group'), axis=0, tiled=False)]
    pallas_call x1 -> x2, Pallas kernels: 79.8 us -> 98.9 us  [the longest x1 49.9 us: solve(): pl.pallas_call(functools.partial(solve_kernel, rows_total, chunk), out_sh...]
    dot_general x1, matrix products: 17.6 us -> 10.3 us  [local(): lax.dot_general(train_grads, train_grads, (((0,), (0,)), ((), ())), preci...]
    reshape x1 -> x0, local copies, waits for them, and re-layouts: 3.15 us -> none  [local(): gathered.reshape(devices, group, per, part, features)]
  transfers between devices with their start and end apart: 2 -> 1, of which waited for: 2 -> 1; matrix products, arithmetic and copies ran while one was open for 7% -> 9% of each run, Pallas kernels for 0% -> 37%
where the time goes in v2:
time: 134 us
  Pallas kernels  98.9 us (74%)
  between operations  15.4 us (11%)
  matrix products  13.7 us (10%)
  local copies, waits for them, and re-layouts  3.28 us (2%)
    pallas_call x1, Pallas kernels, solve(): pl.pallas_call(functools.partial(solve_kernel, rows_total, chunk), out_sh...  49.9 us
    pallas_call x1, Pallas kernels, sum_gram(): pl.pallas_call(functools.partial(sum_kernel, streams), out_shape=jax.Shap...  48.9 us
    dot_general x1, matrix products, local(): lax.dot_general(train_grads, train_grads, (((0,), (0,)), ((), ())), preci...  10.3 us
    dot_general x1, matrix products, local(): lax.dot_general(train_grads, solved, (((1,), (1,)), ((), ())), precision=...  3.35 us
  transfers between devices with their start and end apart: 1, of which 1 were waited for; matrix products, arithmetic and copies ran while one was open for 9% of the time, Pallas kernels for 37%

profile of v2, /device:TPU:0, one launch (start us, length us, event | category | flops | bytes accessed | tf_op | source)
XLA Modules:
  0.0 133.6 jit_solution(977029344649160670)
XLA Ops:
  6.5 0.0 copy-start
  6.5 0.0 all-gather.3.cloned.1.call-start
  6.5 0.7 all-gather.3.cloned.1.call-update
  7.3 1.3 fusion
  10.5 0.0 copy-done
  10.5 0.5 dynamic-slice_bitcast_fusion.request
  11.1 10.3 %fusion.1.gram = f32[1024,1024]{1,0:T(8,128)S(1)} fusion(f32[1024,1024]{1,0:T(8,128)} %param.4), kind=kOutput, calls=%fused_computation.4 | convolution fusion | flops 6442450944 | bytes 8388608 | tf_op jit(solution)/shard_map/dot_general | solution.py:276
  21.4 48.9 %shard_map.46.gram = f32[4608,128]{1,0:T(8,128)S(1)} custom-call(f32[1024,1024]{1,0:T(8,128)S(1)} %fusion.1.gram), custom_call_target="tpu_custom_call" | custom-call | flops 10000000000 | bytes 100000000 | tf_op jit(solution)/shard_map/pallas_call | solution.py:126
  70.3 0.0 copy-start.1
  70.3 1.4 %copy-done.1 = f32[4608,128]{1,0:T(8,128)} copy-done((f32[4608,128]{1,0:T(8,128)}, f32[4608,128]{1,0:T(8,128)S(1)}, u32[]{:S(2)}) %copy-start.1) | copy-done | bytes 2359320
  71.7 0.4 all-gather.3.cloned.1.call-done
  72.1 0.0 copy-start.2
  72.1 49.9 %shard_map.47 = f32[256,1024]{1,0:T(8,128)} custom-call(s32[8]{0:T(128)} %dynamic-slice_bitcast_fusion.request, f32[4608,128]{1,0:T(8,128)} %copy-done.1, f32[8,4,2,8,1024]{4,3,2,1,0:T(8,128)} %bitcast.9), custom_call_target="tpu_custom_call" | custom-call | flops 10000000000 | bytes 10000000 | tf_op jit(solution)/shard_map/pallas_call | solution.py:248
  122.1 0.0 copy-done.2
  122.1 3.3 %convolution_bitcast_fusion = f32[1024,256]{0,1:T(8,128)S(1)} fusion(f32[256,1024]{1,0:T(8,128)} %shard_map.47, f32[1024,1024]{1,0:T(8,128)S(1)} %copy-done.2), kind=kOutput, calls=%fused_computation | convolution fusion | flops 1610612736 | bytes 6291456 | tf_op jit(solution)/shard_map/dot_general | solution.py:287
  125.4 1.3 copy.6
Async XLA Ops:
  6.5 4.0 %copy-start = (s32[8,8]{1,0:T(8,128)S(1)}, s32[8,8]{1,0:T(8,128)}, u32[]{:S(2)}) copy-start(s32[8,8]{1,0:T(8,128)} %param.6) | copy-start | bytes 772
  6.5 65.6 %all-gather.3.cloned.1.call-start = ((), (), s32[]{:S(2)}) async-start(), calls=%async_computation | async-start | bytes 2162688 | tf_op jit(solution)/shard_map/all_gather | solution.py:271
  70.3 1.4 %copy-start.1 = (f32[4608,128]{1,0:T(8,128)}, f32[4608,128]{1,0:T(8,128)S(1)}, u32[]{:S(2)}) copy-start(f32[4608,128]{1,0:T(8,128)S(1)} %shard_map.46.gram) | copy-start | bytes 7077892
  72.1 49.9 %copy-start.2 = (f32[1024,1024]{1,0:T(8,128)S(1)}, f32[1024,1024]{1,0:T(8,128)}, u32[]{:S(2)}) copy-start(f32[1024,1024]{1,0:T(8,128)} %param.4) | copy-start | bytes 12582916
Sparse Core Ops, SparseCore 0:
  10.2 61.8 all-gather.2

commit v3 on v2

--- a/solution.py
+++ b/solution.py
@@ -11,12 +11,19 @@
 BLOCK = 128
 SUB = 8
 STREAMS = 3
+GROUPED = 2
 MESH = pl.DeviceIdType.MESH
 
 
 def upper_blocks(features):
     steps = features // BLOCK
     return [(i, j) for i in range(steps) for j in range(i, steps)]
+
+
+def block_of(strips, i, j):
+    strip, row = strips[i // GROUPED], i % GROUPED
+    col = j - i // GROUPED * GROUPED
+    return strip[row * BLOCK : (row + 1) * BLOCK, col * BLOCK : (col + 1) * BLOCK]
 
 
 def sum_plan(dp, group, features):
@@ -41,8 +48,9 @@
     return mine, {axis: index + weight * (1 - 2 * mine)}
 
 
-def sum_kernel(streams, gram, out, total, landed, send_sem, recv_sem):
-    features = gram.shape[0]
+def sum_kernel(streams, *refs):
+    *gram, out, total, landed, send_sem, recv_sem = refs
+    features = gram[0].shape[1]
     rows = total.shape[0]
     depth = len(streams[0])
     bits = sorted(set(streams[0]))
@@ -50,7 +58,7 @@
     for bit in bits:
         pl.semaphore_signal(barrier, inc=1, device_id=place_of(bit)[1], device_id_type=MESH)
     for n, (i, j) in enumerate(upper_blocks(features)):
-        total[n * BLOCK : (n + 1) * BLOCK, :] = gram[i * BLOCK : (i + 1) * BLOCK, j * BLOCK : (j + 1) * BLOCK]
+        total[n * BLOCK : (n + 1) * BLOCK, :] = block_of(gram, i, j)
     pl.semaphore_wait(barrier, len(bits))
 
     half = rows // 2
@@ -119,14 +127,14 @@
                 backs[s][t - 1].start()
 
 
-def sum_gram(partial_gram, streams):
-    features = partial_gram.shape[0]
+def sum_gram(strips, streams):
+    features = strips[0].shape[1]
     rows = len(upper_blocks(features)) * BLOCK
     depth = len(streams[0])
     return pl.pallas_call(
         functools.partial(sum_kernel, streams),
         out_shape=jax.ShapeDtypeStruct((rows, BLOCK), jnp.float32),
-        in_specs=[pl.BlockSpec(memory_space=pltpu.VMEM)],
+        in_specs=[pl.BlockSpec(memory_space=pltpu.VMEM)] * len(strips),
         out_specs=pl.BlockSpec(memory_space=pltpu.VMEM),
         scratch_shapes=[
             pltpu.VMEM((rows, BLOCK), jnp.float32),
@@ -138,7 +146,14 @@
             collective_id=0, has_side_effects=True, vmem_limit_bytes=24 * 2**20
         ),
         cost_estimate=pl.CostEstimate(flops=10**10, bytes_accessed=10**8, transcendentals=0),
-    )(partial_gram)
+    )(*strips)
+
+
+def reciprocal(x):
+    guess = pl.reciprocal(x, approx=True)
+    for _ in range(2):
+        guess = guess * (2.0 - x * guess)
+    return guess
 
 
 def invert_block(rows):
@@ -152,22 +167,30 @@
         cols = [jnp.broadcast_to(panel[:, base + j : base + j + 1], (SUB, BLOCK)) for j in range(SUB)]
         inside = (lane >= base) & (lane < base + SUB)
         new = jnp.where(inside, jnp.where(lane - base == sub, 1.0, 0.0), panel)
-        for j in range(SUB):
-            inv = 1.0 / cols[j][j : j + 1, :]
-            factor = jnp.where(is_row[j], 0.0, cols[j])
-            pivot = new[j : j + 1, :] * inv
-            for l in range(j + 1, SUB):
-                head = cols[l][j : j + 1, :] * inv
-                cols[l] = jnp.where(is_row[j], head, cols[l]) - factor * head
-            new = jnp.where(is_row[j], pivot, new) - factor * pivot
-        for r in range(BLOCK // SUB):
-            if r == p:
-                continue
+        for j in range(0, SUB, 2):
+            one, two = is_row[j], is_row[j + 1]
+            both = one | two
+            first, second = cols[j], cols[j + 1]
+            aa, ab, bb = first[j : j + 1, :], second[j : j + 1, :], second[j + 1 : j + 2, :]
+            inv = reciprocal(aa * bb - ab * ab)
+            first, second = jnp.where(both, 0.0, first), jnp.where(both, 0.0, second)
+
+            def eliminate(x):
+                top, low = x[j : j + 1, :], x[j + 1 : j + 2, :]
+                top, low = (bb * top - ab * low) * inv, (aa * low - ab * top) * inv
+                kept = jnp.where(one, top, jnp.where(two, low, x))
+                return kept - (first * top + second * low)
+
+            for l in range(j + 2, SUB):
+                cols[l] = eliminate(cols[l])
+            new = eliminate(new)
+        for step in range(1, BLOCK // SUB):
+            r = (p + step) % (BLOCK // SUB)
             old = rows[r]
-            total = jnp.where(inside, 0.0, old)
-            for j in range(SUB):
-                total = total - old[:, base + j : base + j + 1] * new[j : j + 1, :]
-            rows[r] = total
+            terms = [old[:, base + j : base + j + 1] * new[j : j + 1, :] for j in range(SUB)]
+            while len(terms) > 1:
+                terms = [x + y for x, y in zip(terms[::2], terms[1::2])]
+            rows[r] = jnp.where(inside, 0.0, old) - terms[0]
         rows[p] = new
     return rows
 
@@ -217,21 +240,21 @@
         at = pl.ds(pl.multiple_of(k * BLOCK, BLOCK), BLOCK)
         block = work[at, at]
         inverse = jnp.concatenate(invert_block([block[SUB * r : SUB * r + SUB] for r in range(BLOCK // SUB)]), axis=0)
-        scaled[...] = inverse
         col = lax.broadcasted_iota(jnp.int32, (BLOCK, features), 1)
         outside = (col < k * BLOCK) | (col >= (k + 1) * BLOCK)
-        high, low = halves(jnp.where(outside, work[at, :], 0.0))
+        scaled[...] = dot(inverse, jnp.where(outside, work[at, :], 0.0))
+        scaled[:, at] = -inverse
+        high, low = halves(scaled[...])
         right[0:BLOCK, :] = high
         right[BLOCK : 2 * BLOCK, :] = low
         right[2 * BLOCK :, :] = high
 
         def update(i, carry):
             to = pl.ds(pl.multiple_of(i * chunk, chunk), chunk)
-            column = dot(work[to, at], scaled[...])
-            column_high, column_low = halves(column)
-            left = jnp.concatenate([column_high, column_high, column_low], axis=1)
+            high, low = halves(work[to, at])
+            left = jnp.concatenate([high, high, low], axis=1)
+            work[to, at] = jnp.zeros((chunk, BLOCK), jnp.float32)
             work[to, :] -= jnp.dot(left, right[...], preferred_element_type=jnp.float32)
-            work[to, at] = column
             return carry
 
         lax.fori_loop((k + 1) * BLOCK // chunk, work.shape[0] // chunk, update, 0)
@@ -256,7 +279,7 @@
         out_specs=pl.BlockSpec(memory_space=pltpu.VMEM),
         scratch_shapes=[
             pltpu.VMEM((features + slots * vb, features), jnp.float32),
-            pltpu.VMEM((BLOCK, BLOCK), jnp.float32),
+            pltpu.VMEM((BLOCK, features), jnp.float32),
             pltpu.VMEM((3 * BLOCK, features), jnp.bfloat16),
         ],
         compiler_params=pltpu.CompilerParams(vmem_limit_bytes=56 * 2**20),
@@ -273,16 +296,21 @@
     own_index = lax.axis_index("dp")
     mine = jnp.sum(jnp.where(owner == own_index, jnp.arange(devices, dtype=jnp.int32), 0))
     request = lax.dynamic_index_in_dim(wanted, mine, 0, keepdims=False)
-    partial_gram = lax.dot_general(
-        train_grads, train_grads, (((0,), (0,)), ((), ())), precision=lax.Precision.HIGH
-    )
+    strip = GROUPED * BLOCK
+    strips = [
+        lax.dot_general(
+            train_grads[:, start : start + strip],
+            train_grads[:, start:],
+            (((0,), (0,)), ((), ())),
+            precision=lax.Precision.HIGH,
+        )
+        for start in range(0, features, strip)
+    ]
     if streams is None:
-        summed = lax.psum(partial_gram, ("dp", "group"))
-        summed = jnp.concatenate(
-            [summed[i * BLOCK : (i + 1) * BLOCK, j * BLOCK : (j + 1) * BLOCK] for i, j in upper_blocks(features)]
-        )
+        strips = lax.psum(strips, ("dp", "group"))
+        summed = jnp.concatenate([block_of(strips, i, j) for i, j in upper_blocks(features)])
     else:
-        summed = sum_gram(partial_gram, streams)
+        summed = sum_gram(strips, streams)
     solved = solve(summed, blocks, request, rows_total)
     return lax.dot_general(train_grads, solved, (((1,), (1,)), ((), ())), precision=lax.Precision.HIGH)
 

time: 134 us -> 131 us (0.978)
  Pallas kernels: 98.9 us -> 97 us
    pallas_call x1, Pallas kernels: 49.9 us -> 48 us  [solve(): pl.pallas_call(functools.partial(solve_kernel, rows_total, chunk), out_sh...]
    dot_general x1 -> x4, matrix products: 10.3 us -> 9.83 us  [local(): lax.dot_general(train_grads[:, start:start + strip], train_grads[:, start...]
where the time goes in v3:
time: 131 us
  Pallas kernels  97 us (74%)
  between operations  15.4 us (12%)
  matrix products  13.2 us (10%)
  local copies, waits for them, and re-layouts  3.32 us (3%)
    pallas_call x1, Pallas kernels, sum_gram(): pl.pallas_call(functools.partial(sum_kernel, streams), out_shape=jax.Shap...  49.1 us
    pallas_call x1, Pallas kernels, solve(): pl.pallas_call(functools.partial(solve_kernel, rows_total, chunk), out_sh...  48 us
    dot_general x4, matrix products, local(): lax.dot_general(train_grads[:, start:start + strip], train_grads[:, start...  9.83 us
    dot_general x1, matrix products, local(): lax.dot_general(train_grads, solved, (((1,), (1,)), ((), ())), precision=...  3.35 us
  transfers between devices with their start and end apart: 1, of which 1 were waited for; matrix products, arithmetic and copies ran while one was open for 9% of the time, Pallas kernels for 37%

profile of v3, /device:TPU:0, one launch (start us, length us, event | category | flops | bytes accessed | tf_op | source)
XLA Modules:
  0.0 131.1 jit_solution(10879177777178272817)
XLA Ops:
  6.5 0.0 copy-start
  6.5 0.0 all-gather.3.cloned.1.call-start
  6.5 0.7 all-gather.3.cloned.1.call-update
  7.3 1.3 fusion.10
  10.5 0.0 copy-done
  10.5 0.0 copy-start.2
  10.5 0.6 dynamic-slice_bitcast_fusion.request
  11.1 2.8 %fusion.4.refs_3_ = f32[256,256]{1,0:T(8,128)S(1)} fusion(f32[1024,1024]{1,0:T(8,128)} %param.4), kind=kOutput, calls=%fused_computation.5 | convolution fusion | flops 402653184 | bytes 1310720 | tf_op jit(solution)/shard_map/dot_general | solution.py:301
  14.0 3.0 %fusion.2.refs_2_ = f32[256,512]{1,0:T(8,128)S(1)} fusion(f32[1024,1024]{1,0:T(8,128)} %param.4), kind=kOutput, calls=%fused_computation.2 | convolution fusion | flops 805306368 | bytes 3670016 | tf_op jit(solution)/shard_map/dot_general | solution.py:301
  17.0 0.0 copy-done.2
  17.0 1.8 %fusion.refs_1_ = f32[256,768]{1,0:T(8,128)S(1)} fusion(f32[1024,1024]{1,0:T(8,128)S(1)} %copy-done.2), kind=kOutput, calls=%fused_computation | convolution fusion | flops 1207959552 | bytes 4980736 | tf_op jit(solution)/shard_map/dot_general | solution.py:301
  18.8 2.2 %fusion.8.refs_0_ = f32[256,1024]{1,0:T(8,128)S(1)} fusion(f32[1024,1024]{1,0:T(8,128)S(1)} %copy-done.2), kind=kOutput, calls=%fused_computation.9 | convolution fusion | flops 1610612736 | bytes 6291456 | tf_op jit(solution)/shard_map/dot_general | solution.py:301
  21.0 49.1 %shard_map.46.gram = f32[4608,128]{1,0:T(8,128)S(1)} custom-call(f32[256,1024]{1,0:T(8,128)S(1)} %fusion.8.refs_0_, f32[256,768]{1,0:T(8,128)S(1)} %fusion.refs_1_, f32[256,512]{1,0:T(8,128)S(1)} %fusion.2.refs_2_, f32[256,256]{1,0:T(8,128)S(1)} %fusion.4.refs_3_), custom_call_target="tpu_custom_call" | custom-call | flops 10000000000 | bytes 100000000 | tf_op jit(solution)/shard_map/pallas_call | solution.py:134
  70.1 0.0 copy-start.1
  70.1 1.4 %copy-done.1 = f32[4608,128]{1,0:T(8,128)} copy-done((f32[4608,128]{1,0:T(8,128)}, f32[4608,128]{1,0:T(8,128)S(1)}, u32[]{:S(2)}) %copy-start.1) | copy-done | bytes 2359320
  71.5 0.1 all-gather.3.cloned.1.call-done
  71.6 0.0 copy-start.3
  71.6 48.0 %shard_map.47 = f32[256,1024]{1,0:T(8,128)} custom-call(s32[8]{0:T(128)} %dynamic-slice_bitcast_fusion.request, f32[4608,128]{1,0:T(8,128)} %copy-done.1, f32[8,4,2,8,1024]{4,3,2,1,0:T(8,128)} %bitcast.8), custom_call_target="tpu_custom_call" | custom-call | flops 10000000000 | bytes 10000000 | tf_op jit(solution)/shard_map/pallas_call | solution.py:271
  119.6 0.0 copy-done.3
  119.6 3.3 %convolution_bitcast_fusion = f32[1024,256]{0,1:T(8,128)S(1)} fusion(f32[256,1024]{1,0:T(8,128)} %shard_map.47, f32[1024,1024]{1,0:T(8,128)S(1)} %copy-done.3), kind=kOutput, calls=%fused_computation.4 | convolution fusion | flops 1610612736 | bytes 6291456 | tf_op jit(solution)/shard_map/dot_general | solution.py:315
  122.9 1.3 copy.6
Async XLA Ops:
  6.5 4.0 %copy-start = (s32[8,8]{1,0:T(8,128)S(1)}, s32[8,8]{1,0:T(8,128)}, u32[]{:S(2)}) copy-start(s32[8,8]{1,0:T(8,128)} %param.6) | copy-start | bytes 772
  6.5 65.1 %all-gather.3.cloned.1.call-start = ((), (), s32[]{:S(2)}) async-start(), calls=%async_computation | async-start | bytes 2162688 | tf_op jit(solution)/shard_map/all_gather | solution.py:294
  10.5 6.5 %copy-start.2 = (f32[1024,1024]{1,0:T(8,128)S(1)}, f32[1024,1024]{1,0:T(8,128)}, u32[]{:S(2)}) copy-start(f32[1024,1024]{1,0:T(8,128)} %param.4) | copy-start | bytes 12582916
  70.1 1.4 %copy-start.1 = (f32[4608,128]{1,0:T(8,128)}, f32[4608,128]{1,0:T(8,128)S(1)}, u32[]{:S(2)}) copy-start(f32[4608,128]{1,0:T(8,128)S(1)} %shard_map.46.gram) | copy-start | bytes 7077892
  71.6 48.0 %copy-start.3 = (f32[1024,1024]{1,0:T(8,128)S(1)}, f32[1024,1024]{1,0:T(8,128)}, u32[]{:S(2)}) copy-start(f32[1024,1024]{1,0:T(8,128)} %param.4) | copy-start | bytes 12582916
Sparse Core Ops, SparseCore 0:
  10.2 61.3 all-gather.2

commit v4 on v3

--- a/solution.py
+++ b/solution.py
@@ -49,7 +49,7 @@
 
 
 def sum_kernel(streams, *refs):
-    *gram, out, total, landed, send_sem, recv_sem = refs
+    own, *gram, out, vals, total, landed, send_sem, recv_sem, val_send, val_recv = refs
     features = gram[0].shape[1]
     rows = total.shape[0]
     depth = len(streams[0])
@@ -57,6 +57,25 @@
     barrier = pltpu.get_barrier_semaphore()
     for bit in bits:
         pl.semaphore_signal(barrier, inc=1, device_id=place_of(bit)[1], device_id_type=MESH)
+    val_held, place, span = [], 0, vals.shape[0]
+    for bit in streams[0]:
+        span = span // 2
+        place = place + place_of(bit)[0] * span
+        val_held.append((place, span))
+    vals[pl.ds(place, 1)] = own[...][None]
+
+    def val_copy(t):
+        return pltpu.make_async_remote_copy(
+            src_ref=vals.at[pl.ds(*val_held[t])],
+            dst_ref=vals.at[pl.ds(*val_held[t])],
+            send_sem=val_send.at[t],
+            recv_sem=val_recv.at[t],
+            device_id=place_of(streams[0][t])[1],
+            device_id_type=MESH,
+        )
+
+    val_copies = [val_copy(t) for t in reversed(range(depth))]
+    val_waits = (1, 2, 4, 6)
     for n, (i, j) in enumerate(upper_blocks(features)):
         total[n * BLOCK : (n + 1) * BLOCK, :] = block_of(gram, i, j)
     pl.semaphore_wait(barrier, len(bits))
@@ -110,6 +129,8 @@
     backs = [[back_copy(s, t) for t in range(depth)] for s in range(len(streams))]
     for s in range(len(streams)):
         outs[s][0].start()
+    val_copies[0].start()
+    val_done = 0
     for t in range(depth):
         for s in range(len(streams)):
             outs[s][t].wait()
@@ -120,33 +141,51 @@
             else:
                 out[here, :] = total[here, :] + landed[pl.ds(*slot[s][t]), :]
                 backs[s][t].start()
+        if t in val_waits and val_done + 1 < depth:
+            val_copies[val_done].wait()
+            val_done += 1
+            val_copies[val_done].start()
     for t in reversed(range(depth)):
         for s in range(len(streams)):
             backs[s][t].wait()
             if t > 0:
                 backs[s][t - 1].start()
-
-
-def sum_gram(strips, streams):
+        if 2 * depth - 1 - t in val_waits and val_done + 1 < depth:
+            val_copies[val_done].wait()
+            val_done += 1
+            val_copies[val_done].start()
+    while val_done < depth:
+        val_copies[val_done].wait()
+        val_done += 1
+        if val_done < depth:
+            val_copies[val_done].start()
+
+
+def sum_gram(val_grads, strips, streams):
     features = strips[0].shape[1]
     rows = len(upper_blocks(features)) * BLOCK
     depth = len(streams[0])
     return pl.pallas_call(
         functools.partial(sum_kernel, streams),
-        out_shape=jax.ShapeDtypeStruct((rows, BLOCK), jnp.float32),
-        in_specs=[pl.BlockSpec(memory_space=pltpu.VMEM)] * len(strips),
-        out_specs=pl.BlockSpec(memory_space=pltpu.VMEM),
+        out_shape=[
+            jax.ShapeDtypeStruct((rows, BLOCK), jnp.float32),
+            jax.ShapeDtypeStruct((1 << depth,) + val_grads.shape, jnp.float32),
+        ],
+        in_specs=[pl.BlockSpec(memory_space=pltpu.VMEM)] * (1 + len(strips)),
+        out_specs=[pl.BlockSpec(memory_space=pltpu.VMEM)] * 2,
         scratch_shapes=[
             pltpu.VMEM((rows, BLOCK), jnp.float32),
             pltpu.VMEM((rows, BLOCK), jnp.float32),
             pltpu.SemaphoreType.DMA((2, STREAMS, depth)),
             pltpu.SemaphoreType.DMA((2, STREAMS, depth)),
+            pltpu.SemaphoreType.DMA((depth,)),
+            pltpu.SemaphoreType.DMA((depth,)),
         ],
         compiler_params=pltpu.CompilerParams(
             collective_id=0, has_side_effects=True, vmem_limit_bytes=24 * 2**20
         ),
         cost_estimate=pl.CostEstimate(flops=10**10, bytes_accessed=10**8, transcendentals=0),
-    )(*strips)
+    )(val_grads, *strips)
 
 
 def reciprocal(x):
@@ -208,12 +247,21 @@
     return jnp.dot(left, right, preferred_element_type=jnp.float32)
 
 
-def solve_kernel(rows_total, chunk, request, gram, blocks, out, work, scaled, right):
+def piece_of(d, g, group, order):
+    if order is None:
+        return d * group + g
+    place = 0
+    for axis, weight in order:
+        place = 2 * place + (g // weight % 2 if axis == "group" else lax.rem(lax.div(d, weight), 2))
+    return place
+
+
+def solve_kernel(rows_total, chunk, order, group, request, gram, blocks, out, work, scaled, right):
     features = out.shape[1]
     steps = features // BLOCK
     slots = request.shape[0]
-    part = blocks.shape[3]
-    vb = blocks.shape[1] * part
+    per, part = blocks.shape[1], blocks.shape[2]
+    vb = group * part
     scale = features ** (-0.5)
     diagonal = lax.broadcasted_iota(jnp.int32, (BLOCK, BLOCK), 0) == lax.broadcasted_iota(jnp.int32, (BLOCK, BLOCK), 1)
     for n, (i, j) in enumerate(upper_blocks(features)):
@@ -228,10 +276,10 @@
         w = request[j]
         live = jnp.where(w >= 0, scale, 0.0).astype(jnp.float32)
         known = jnp.maximum(w, 0)
-        holder, inner = lax.div(known, blocks.shape[2]), lax.rem(known, blocks.shape[2])
-        for g in range(blocks.shape[1]):
+        holder, inner = lax.div(known, per), lax.rem(known, per)
+        for g in range(group):
             to = pl.ds(pl.multiple_of(features + j * vb + g * part, part), part)
-            work[to, :] = blocks[holder, g, inner] * live
+            work[to, :] = blocks[piece_of(holder, g, group, order), inner] * live
         return carry
 
     lax.fori_loop(0, slots, pick, 0)
@@ -264,12 +312,12 @@
     out[...] = work[features:, :]
 
 
-def solve(gram_sum, blocks, request, rows_total):
-    features = blocks.shape[4]
-    slots, vb = request.shape[0], blocks.shape[1] * blocks.shape[3]
+def solve(gram_sum, blocks, request, rows_total, order, group):
+    features = blocks.shape[3]
+    slots, vb = request.shape[0], group * blocks.shape[2]
     chunk = 2 * BLOCK
     return pl.pallas_call(
-        functools.partial(solve_kernel, rows_total, chunk),
+        functools.partial(solve_kernel, rows_total, chunk, order, group),
         out_shape=jax.ShapeDtypeStruct((slots * vb, features), jnp.float32),
         in_specs=[
             pl.BlockSpec(memory_space=pltpu.SMEM),
@@ -291,8 +339,6 @@
     features = train_grads.shape[1]
     devices, group = lax.axis_size("dp"), lax.axis_size("group")
     rows_total = train_grads.shape[0] * devices * group
-    gathered = lax.all_gather(val_grads, ("dp", "group"), axis=0, tiled=False)
-    blocks = gathered.reshape((devices, group) + val_grads.shape)
     own_index = lax.axis_index("dp")
     mine = jnp.sum(jnp.where(owner == own_index, jnp.arange(devices, dtype=jnp.int32), 0))
     request = lax.dynamic_index_in_dim(wanted, mine, 0, keepdims=False)
@@ -307,11 +353,14 @@
         for start in range(0, features, strip)
     ]
     if streams is None:
+        order = None
+        blocks = lax.all_gather(val_grads, ("dp", "group"), axis=0, tiled=False)
         strips = lax.psum(strips, ("dp", "group"))
         summed = jnp.concatenate([block_of(strips, i, j) for i, j in upper_blocks(features)])
     else:
-        summed = sum_gram(strips, streams)
-    solved = solve(summed, blocks, request, rows_total)
+        order = streams[0]
+        summed, blocks = sum_gram(val_grads, strips, streams)
+    solved = solve(summed, blocks, request, rows_total, order, group)
     return lax.dot_general(train_grads, solved, (((1,), (1,)), ((), ())), precision=lax.Precision.HIGH)
 
 

time: 131 us -> 121 us (0.924)
  between operations: 15.4 us -> 2.04 us
  Pallas kernels: 97 us -> 99.3 us
    pallas_call x2, Pallas kernels: 97 us -> 99.3 us  [the longest x1 51.5 us: sum_gram(): pl.pallas_call(functools.partial(sum_kernel, streams), out_shape=[jax.Sha...]
    unnamed x8 -> x10, local copies, waits for them, and re-layouts: 1.43 us -> 2.75 us
  transfers between devices with their start and end apart: 1 -> 0, of which waited for: 1 -> 0; matrix products, arithmetic and copies ran while one was open for 9% -> 0% of each run, Pallas kernels for 37% -> 0%
where the time goes in v4:
time: 121 us; the launch traced here: 120 us
  Pallas kernels  99.3 us (82%)
  matrix products  13.1 us (11%)
  local copies, waits for them, and re-layouts  4.6 us (4%)
  between operations  2.04 us (2%)
  other arithmetic  1.3 us (1%)
    pallas_call x1, Pallas kernels, sum_gram(): pl.pallas_call(functools.partial(sum_kernel, streams), out_shape=[jax.Sha...  51.5 us
    pallas_call x1, Pallas kernels, solve(): pl.pallas_call(functools.partial(solve_kernel, rows_total, chunk, order,...  47.9 us
    dot_general x4, matrix products, local(): lax.dot_general(train_grads[:, start:start + strip], train_grads[:, start...  9.77 us
    dot_general x1, matrix products, local(): lax.dot_general(train_grads, solved, (((1,), (1,)), ((), ())), precision=...  3.35 us
    unnamed x10, local copies, waits for them, and re-layouts  2.75 us

profile of v4, /device:TPU:0, one launch (start us, length us, event | category | flops | bytes accessed | tf_op | source)
XLA Modules:
  0.0 120.4 jit_solution(15087801007565605176)
XLA Ops:
  0.0 0.0 copy-start
  0.0 1.3 %fusion.10 = s32[]{:T(128)} fusion(s32[8]{0:T(128)} %param.7, s32[]{:T(128)S(6)} %axis_index.15), kind=kLoop, calls=%fused_computation.12 | loop fusion | flops 23 | bytes 40 | tf_op jit(solution)/shard_map/reduce_sum | solution.py:343
  3.3 0.0 copy-done
  3.3 0.0 copy-start.4
  3.3 0.5 dynamic-slice_bitcast_fusion.request
  3.8 2.8 %fusion.4.refs_4_ = f32[256,256]{1,0:T(8,128)S(1)} fusion(f32[1024,1024]{1,0:T(8,128)} %param.4), kind=kOutput, calls=%fused_computation.5 | convolution fusion | flops 402653184 | bytes 1310720 | tf_op jit(solution)/shard_map/dot_general | solution.py:347
  6.6 3.0 %fusion.2.refs_3_ = f32[256,512]{1,0:T(8,128)S(1)} fusion(f32[1024,1024]{1,0:T(8,128)} %param.4), kind=kOutput, calls=%fused_computation.2 | convolution fusion | flops 805306368 | bytes 3670016 | tf_op jit(solution)/shard_map/dot_general | solution.py:347
  9.7 0.0 copy-done.4
  9.7 1.8 %fusion.refs_2_ = f32[256,768]{1,0:T(8,128)S(1)} fusion(f32[1024,1024]{1,0:T(8,128)S(1)} %copy-done.4), kind=kOutput, calls=%fused_computation | convolution fusion | flops 1207959552 | bytes 4980736 | tf_op jit(solution)/shard_map/dot_general | solution.py:347
  11.5 0.0 copy-start.1
  11.5 2.1 %fusion.8.refs_1_ = f32[256,1024]{1,0:T(8,128)S(1)} fusion(f32[1024,1024]{1,0:T(8,128)S(1)} %copy-done.4), kind=kOutput, calls=%fused_computation.9 | convolution fusion | flops 1610612736 | bytes 6291456 | tf_op jit(solution)/shard_map/dot_general | solution.py:347
  13.6 0.0 copy-done.1
  13.7 51.5 %shard_map.46 = (f32[4608,128]{1,0:T(8,128)S(1)}, f32[32,2,8,1024]{3,2,1,0:T(8,128)S(1)}) custom-call(f32[2,8,1024]{2,1,0:T(8,128)S(1)} %copy-done.1, f32[256,1024]{1,0:T(8,128)S(1)} %fusion.8.refs_1_, f32[256,768]{1,0:T(8,128)S(1)} %fusion.refs_2_, f32[256,512]{1,0:T(8,128)S(1)} %fusion.2.refs_3_, f32[256,256]{1,0:T(8,128)S(1)} %fusion.4.refs_4_), custom_call_target="tpu_custom_call" | custom-call | flops 10000000000 | bytes 100000000 | tf_op jit(solution)/shard_map/pallas_call | solution.py:168
  65.1 0.0 copy-start.2
  65.1 1.4 %copy-done.2 = f32[4608,128]{1,0:T(8,128)} copy-done((f32[4608,128]{1,0:T(8,128)}, f32[4608,128]{1,0:T(8,128)S(1)}, u32[]{:S(2)}) %copy-start.2) | copy-done | bytes 2359320
  66.5 0.0 copy-start.3
  66.5 1.3 %copy-done.3 = f32[32,2,8,1024]{3,2,1,0:T(8,128)} copy-done((f32[32,2,8,1024]{3,2,1,0:T(8,128)}, f32[32,2,8,1024]{3,2,1,0:T(8,128)S(1)}, u32[]{:S(2)}) %copy-start.3) | copy-done | bytes 2097176
  67.9 47.9 %shard_map.47 = f32[256,1024]{1,0:T(8,128)} custom-call(s32[8]{0:T(128)} %dynamic-slice_bitcast_fusion.request, f32[4608,128]{1,0:T(8,128)} %copy-done.2, f32[32,2,8,1024]{3,2,1,0:T(8,128)} %copy-done.3), custom_call_target="tpu_custom_call" | custom-call | flops 10000000000 | bytes 10000000 | tf_op jit(solution)/shard_map/pallas_call | solution.py:319
  115.7 3.3 %convolution_bitcast_fusion = f32[1024,256]{0,1:T(8,128)S(1)} fusion(f32[256,1024]{1,0:T(8,128)} %shard_map.47, f32[1024,1024]{1,0:T(8,128)S(1)} %copy-done.4), kind=kOutput, calls=%fused_computation.4 | convolution fusion | flops 1610612736 | bytes 6291456 | tf_op jit(solution)/shard_map/dot_general | solution.py:364
  119.1 1.3 %copy.5 = f32[1024,256]{1,0:T(8,128)} copy(f32[1024,256]{0,1:T(8,128)S(1)} %convolution_bitcast_fusion) | data formatting | bytes 2097152 | tf_op jit(solution)/shard_map/dot_general | solution.py:364
Async XLA Ops:
  0.0 3.3 %copy-start = (s32[8,8]{1,0:T(8,128)S(1)}, s32[8,8]{1,0:T(8,128)}, u32[]{:S(2)}) copy-start(s32[8,8]{1,0:T(8,128)} %param.6) | copy-start | bytes 772
  3.3 6.4 %copy-start.4 = (f32[1024,1024]{1,0:T(8,128)S(1)}, f32[1024,1024]{1,0:T(8,128)}, u32[]{:S(2)}) copy-start(f32[1024,1024]{1,0:T(8,128)} %param.4) | copy-start | bytes 12582916
  11.5 2.2 %copy-start.1 = (f32[2,8,1024]{2,1,0:T(8,128)S(1)}, f32[2,8,1024]{2,1,0:T(8,128)}, u32[]{:S(2)}) copy-start(f32[2,8,1024]{2,1,0:T(8,128)} %refs_0_.1) | copy-start | bytes 196612
  65.1 1.4 %copy-start.2 = (f32[4608,128]{1,0:T(8,128)}, f32[4608,128]{1,0:T(8,128)S(1)}, u32[]{:S(2)}) copy-start(f32[4608,128]{1,0:T(8,128)S(1)} %get-tuple-element.7.gram) | copy-start | bytes 7077892
  66.5 1.3 %copy-start.3 = (f32[32,2,8,1024]{3,2,1,0:T(8,128)}, f32[32,2,8,1024]{3,2,1,0:T(8,128)S(1)}, u32[]{:S(2)}) copy-start(f32[32,2,8,1024]{3,2,1,0:T(8,128)S(1)} %get-tuple-element.8.blocks) | copy-start | bytes 6291460
